TPU v7x, 128 devices: a whole 4x4x4 slice. The times are simulated.
128 devices in a mesh: row: 8 (over y, z_lo), col: 16 (over z_hi, x, core).
Axes of the slice: x: 4, y: 4, z: 4 (z_hi: 2, z_lo: 2; z = z_hi * 2 + z_lo), core: 2. Of those that a mesh axis runs over, the one named last changes fastest.
Arguments:
- a_values: bfloat16 [64, 16, 128, 128], P('row', 'col'), may hold values from -6 to 6
- a_blocks: int32 [64, 16], P('row', 'col'), may hold values from 0 to 511, as said below
- a_live: int32 [64, 16], P('row', 'col'), may hold values from 0 to 1, as said below
- b_values: bfloat16 [512, 16, 128, 128], P('row', 'col'), may hold values from -0.5 to 0.5
- b_columns: int32 [512, 16], P('row', 'col'), may hold values from 0 to 1023, as said below
- filter_mask: int32 [64, 1024], P('row', 'col'), may hold values 0 or 1
Outputs:
- product: bfloat16 [64, 1024, 128, 128], P('row', 'col')
Inputs may be any that keep to these rules, and one draw needn't show every extreme that they name: `a_blocks`: the 16 entries of a block row are distinct. `a_live`: every block row has at least one live slot; some block row has all 16 live. `b_columns`: in a contraction row, slot g names a block column between g * 64 and (g + 1) * 64 - 1, so the slot held by index g of col always falls in that index's block columns.
All inputs are finite; a program needn't handle non-finite values. No bound on the sum of `filter_mask` on one device may be relied on, other than what follows from the above.
Results may differ from a plain program's by a relative error of at most 0.001.
Values may be sent and summed in bfloat16 or wider, within the bound.
No kernel may reach another device: no remote copies, remote signals or barrier semaphores. Data moves between devices by JAX's collectives and lax.ppermute only.
A program may use at most 192 MiB of HBM per device.

v0:
```python
import jax
import jax.numpy as jnp
from jax import lax
from jax.sharding import PartitionSpec as P


def per_device(a_values, a_blocks, a_live, b_values, b_columns, filter_mask):
    col_count = filter_mask.shape[1]
    b_all, b_cols = (
        lax.all_gather(b_values, "row", axis=0, tiled=True),
        lax.all_gather(b_columns, "row", axis=0, tiled=True),
    )
    local_cols = b_cols - lax.axis_index("col") * col_count
    placed = (local_cols[:, :, None] == jnp.arange(col_count)[None, None, :]).astype(jnp.float32)
    all_values, all_blocks, all_alive = (
        lax.all_gather(a_values, "col", axis=1, tiled=True),
        lax.all_gather(a_blocks, "col", axis=1, tiled=True),
        lax.all_gather(a_live, "col", axis=1, tiled=True),
    )

    def one_row(element):
        values_row, blocks_row, alive_row = element
        chosen = b_all[blocks_row]
        weights = placed[blocks_row] * alive_row.astype(jnp.float32)[:, None, None]
        products = jnp.einsum(
            "amn,abnp->abmp", values_row, chosen, preferred_element_type=jnp.float32
        )
        return jnp.einsum("abj,abmp->jmp", weights, products, precision=lax.Precision.HIGHEST)

    summed = lax.map(one_row, (all_values, all_blocks, all_alive))
    return (summed * filter_mask.astype(jnp.float32)[:, :, None, None]).astype(jnp.bfloat16)


def solution(mesh):
    in_specs = (
        P("row", "col", None, None),
        P("row", "col"),
        P("row", "col"),
        P("row", "col", None, None),
        P("row", "col"),
        P("row", "col"),
    )
    out_specs = P("row", "col", None, None)
    return jax.shard_map(
        per_device, mesh=mesh, in_specs=in_specs, out_specs=out_specs, check_vma=False
    )
```

profile of v0, /device:TPU:1, one launch (start us, length us, event | category | flops | bytes accessed | tf_op | source)
XLA Modules:
  0.0 557.2 jit_solution(8753298809779043239)
XLA Ops:
  8.0 26.4 %all-gather = s32[16,1,8]{2,1,0:T(1,128)S(1)} all-gather(s32[1,1,8]{2,1,0:T(1,128)} %bitcast.73), channel_id=1, replica_groups=mesh['row'=8,'col'=16] {'col'}, dimensions={0}, use_global_device_ids=true | all-gather | bytes 544 | tf_op jit(solution)/shard_map/all_gather | solution.py:17
  34.5 19.3 %all-gather.1 = s32[16,1,8]{2,1,0:T(1,128)S(1)} all-gather(s32[1,1,8]{2,1,0:T(1,128)} %bitcast.74), channel_id=1, replica_groups=mesh['row'=8,'col'=16] {'col'}, dimensions={0}, use_global_device_ids=true | all-gather | bytes 544 | tf_op jit(solution)/shard_map/all_gather | solution.py:18
  57.2 9.8 %all-reduce = s32[512]{0:T(512)S(1)} all-reduce(s32[512]{0:T(512)S(1)} %bitcast_dynamic-update-slice_fusion), channel_id=1, replica_groups=mesh['row'=8,'col'=16] {'row'}, use_global_device_ids=true, to_apply=%add | all-reduce | flops 512 | bytes 4096
  67.0 2.6 all-gather.7.cloned.1.call-done
  69.6 325.6 %all-gather.5.cloned.1.call-done = bf16[512,1,128,128]{3,2,1,0:T(8,128)(2,1)} async-done(((bf16[64,1,128,128]{3,2,1,0:T(8,128)(2,1)}), bf16[512,1,128,128]{3,2,1,0:T(8,128)(2,1)}) %all-gather.5.cloned.1.call-update) | async-done | bytes 16777232 | tf_op jit(solution)/shard_map/all_gather | solution.py:10
  395.2 137.3 %while.11 = (s32[]{:T(128)}, f32[8,64,128,128]{3,2,1,0:T(8,128)}, s32[8,16]{1,0:T(8,128)S(1)}, s32[8,16]{1,0:T(8,128)S(1)}, bf16[512,1,128,128]{3,2,1,0:T(8,128)...) while((s32[]{:T(128)}, f32[8,64,128,128]{3,2,1,0:T(8,128)}, ...), condition=%wide.region_1.2_spmd.clone, body=%wide.region_0.1_spmd.clone.sunk | while | flops 268503104 | bytes 19025500 | solution.py:30
  395.3 6.4 %gather_fusion = bf16[16,128,128]{2,1,0:T(8,128)(2,1)S(1)} fusion(bf16[512,128,128]{2,1,0:T(8,128)(2,1)} %bitcast.70, s32[1024]{0:T(1024)S(1)} %pad_clamp_fusion.2), kind=kCustom, calls=%fused_computation.1.clone.clone.1 | custom fusion | bytes 1048640 | tf_op jit(solution)/shard_map/while/body/eval_jaxpr/gather | solution.py:23
  404.5 3.5 convolution_bitcast_fusion.5
  408.0 4.4 copy_dynamic-update-slice_fusion.2
  412.4 6.4 %gather_fusion = bf16[16,128,128]{2,1,0:T(8,128)(2,1)S(1)} fusion(bf16[512,128,128]{2,1,0:T(8,128)(2,1)} %bitcast.70, s32[1024]{0:T(1024)S(1)} %pad_clamp_fusion.2), kind=kCustom, calls=%fused_computation.1.clone.clone.1 | custom fusion | bytes 1048640 | tf_op jit(solution)/shard_map/while/body/eval_jaxpr/gather | solution.py:23
  421.6 3.5 convolution_bitcast_fusion.5
  425.2 4.4 copy_dynamic-update-slice_fusion.2
  429.6 6.4 %gather_fusion = bf16[16,128,128]{2,1,0:T(8,128)(2,1)S(1)} fusion(bf16[512,128,128]{2,1,0:T(8,128)(2,1)} %bitcast.70, s32[1024]{0:T(1024)S(1)} %pad_clamp_fusion.2), kind=kCustom, calls=%fused_computation.1.clone.clone.1 | custom fusion | bytes 1048640 | tf_op jit(solution)/shard_map/while/body/eval_jaxpr/gather | solution.py:23
  438.8 3.5 convolution_bitcast_fusion.5
  442.3 4.4 copy_dynamic-update-slice_fusion.2
  446.7 6.4 %gather_fusion = bf16[16,128,128]{2,1,0:T(8,128)(2,1)S(1)} fusion(bf16[512,128,128]{2,1,0:T(8,128)(2,1)} %bitcast.70, s32[1024]{0:T(1024)S(1)} %pad_clamp_fusion.2), kind=kCustom, calls=%fused_computation.1.clone.clone.1 | custom fusion | bytes 1048640 | tf_op jit(solution)/shard_map/while/body/eval_jaxpr/gather | solution.py:23
  456.0 3.5 convolution_bitcast_fusion.5
  459.5 4.4 copy_dynamic-update-slice_fusion.2
  463.9 6.4 %gather_fusion = bf16[16,128,128]{2,1,0:T(8,128)(2,1)S(1)} fusion(bf16[512,128,128]{2,1,0:T(8,128)(2,1)} %bitcast.70, s32[1024]{0:T(1024)S(1)} %pad_clamp_fusion.2), kind=kCustom, calls=%fused_computation.1.clone.clone.1 | custom fusion | bytes 1048640 | tf_op jit(solution)/shard_map/while/body/eval_jaxpr/gather | solution.py:23
  473.1 3.5 convolution_bitcast_fusion.5
  476.7 4.4 copy_dynamic-update-slice_fusion.2
  481.0 6.4 %gather_fusion = bf16[16,128,128]{2,1,0:T(8,128)(2,1)S(1)} fusion(bf16[512,128,128]{2,1,0:T(8,128)(2,1)} %bitcast.70, s32[1024]{0:T(1024)S(1)} %pad_clamp_fusion.2), kind=kCustom, calls=%fused_computation.1.clone.clone.1 | custom fusion | bytes 1048640 | tf_op jit(solution)/shard_map/while/body/eval_jaxpr/gather | solution.py:23
  490.3 3.5 convolution_bitcast_fusion.5
  493.8 4.4 copy_dynamic-update-slice_fusion.2
  498.2 6.4 %gather_fusion = bf16[16,128,128]{2,1,0:T(8,128)(2,1)S(1)} fusion(bf16[512,128,128]{2,1,0:T(8,128)(2,1)} %bitcast.70, s32[1024]{0:T(1024)S(1)} %pad_clamp_fusion.2), kind=kCustom, calls=%fused_computation.1.clone.clone.1 | custom fusion | bytes 1048640 | tf_op jit(solution)/shard_map/while/body/eval_jaxpr/gather | solution.py:23
  507.4 3.5 convolution_bitcast_fusion.5
  511.0 4.4 copy_dynamic-update-slice_fusion.2
  515.4 6.4 %gather_fusion = bf16[16,128,128]{2,1,0:T(8,128)(2,1)S(1)} fusion(bf16[512,128,128]{2,1,0:T(8,128)(2,1)} %bitcast.70, s32[1024]{0:T(1024)S(1)} %pad_clamp_fusion.2), kind=kCustom, calls=%fused_computation.1.clone.clone.1 | custom fusion | bytes 1048640 | tf_op jit(solution)/shard_map/while/body/eval_jaxpr/gather | solution.py:23
  521.8 1.6 convolution_bitcast_fusion.4
  524.6 3.5 convolution_bitcast_fusion.5
  528.1 4.4 copy_dynamic-update-slice_fusion.2
  532.5 17.8 %multiply_convert_fusion = bf16[8,64,128,128]{3,2,1,0:T(8,128)(2,1)} fusion(f32[8,64,128,128]{3,2,1,0:T(8,128)} %get-tuple-element.42, f32[8,64]{1,0:T(8,128)S(1)} %convert_element_type.28), kind=kLoop, calls=%fused_computation.22 | loop fusion | flops 16777216 | bytes 50333696 | tf_op jit(solution)/shard_map/convert_element_type | solution.py:31
  (67 shorter events, 25.1 us)
Async XLA Ops:
  6.5 63.1 %all-gather.7.cloned.1.call-start = ((), (), s32[]{:S(2)}) async-start(), calls=%async_computation.1 | async-start | bytes 4456448 | tf_op jit(solution)/shard_map/all_gather | solution.py:16
  7.3 388.0 %all-gather.5.cloned.1.call-start = ((), (), s32[]{:S(2)}) async-start(), calls=%async_computation | async-start | bytes 18874368 | tf_op jit(solution)/shard_map/all_gather | solution.py:10
Sparse Core Ops, SparseCore 0:
  9.8 59.7 all-gather.6
  71.3 323.9 all-gather.4
where the time goes:
time: 558 us; the launch traced here: 557 us
  waiting for transfers between devices  330 us (59%)
  local copies, waits for them, and re-layouts  97.1 us (17%)
  blocking collectives  55.5 us (10%)
  matrix products  40.7 us (7%)
  other arithmetic  19.8 us (4%)
  between operations  14.1 us (3%)
    all_gather x1, waiting for transfers between devices, per_device(): lax.all_gather(b_values, 'row', axis=0, tiled=True)  326 us
    gather x8, local copies, waits for them, and re-layouts, one_row(): chosen = b_all[blocks_row]  51.3 us
    dynamic_update_slice x8, local copies, waits for them, and re-layouts, per_device(): summed = lax.map(one_row, (all_values, all_blocks, all_alive))  35 us
    dot_general x8, matrix products, one_row(): jnp.einsum('abj,abmp->jmp', weights, products, precision=lax.Precision.HI...  28.2 us
    all_gather x1, blocking collectives, per_device(): lax.all_gather(a_blocks, 'col', axis=1, tiled=True)  26.4 us
    all_gather x1, blocking collectives, per_device(): lax.all_gather(a_live, 'col', axis=1, tiled=True)  19.3 us
    convert_element_type x1, other arithmetic, per_device(): (summed * filter_mask.astype(jnp.float32)[:, :, None, None]).astype(jnp.b...  17.8 us
    dot_general x8, matrix products, one_row(): jnp.einsum('amn,abnp->abmp', values_row, chosen, preferred_element_type=j...  12.5 us
  transfers between devices with their start and end apart: 2, of which 2 were waited for; matrix products, arithmetic and copies ran while one was open for 1% of the time, Pallas kernels for 0%

commit v1 on v0

v1 whole, which is shorter than its diff:
```python
import functools

import jax
import jax.numpy as jnp
from jax import lax
from jax.experimental import pallas as pl
from jax.experimental.pallas import tpu as pltpu
from jax.sharding import Mesh, PartitionSpec as P

BS = 128
ROWS = 8
COLS = 16
RB = 8
KB = 64
JB = 64
SLOTS = 16
LANES = 128
CAPS = (12, 14, 16, 18, 20)
R_AXES = ("y", "zl")
C_AXES = ("zh", "x", "core")

SEND = 0
META = 8
KEYS = 16
RANK = 32
MISC = 36
INFO = 40

LEFT, SOURCE, PLACE, COL, HEAD, COUNT = 0, 16, 32, 48, 64, 96
UNROLL = 4


def list_kernel(me_ref, meta_ref, info_ref, which_ref):
    me_r, me_c = me_ref[0], me_ref[1]
    lane = lax.broadcasted_iota(jnp.int32, (LANES, LANES), 1)
    sub8 = lax.broadcasted_iota(jnp.int32, (ROWS, LANES), 0)
    lane8 = lax.broadcasted_iota(jnp.int32, (ROWS, LANES), 1)
    tri_a = lax.broadcasted_iota(jnp.int32, (LANES, LANES), 0)
    before = ((tri_a < lane) & (tri_a // KB == lane // KB)).astype(jnp.float32)
    keys = meta_ref[:, 0:RB]
    top = jnp.zeros((ROWS, LANES), jnp.int32)

    def needed(base):
        hit = jnp.zeros((LANES, LANES), jnp.int32)
        for i in range(RB):
            hit = jnp.where(keys[:, i:i + 1] == lane + base, 1, hit)
        need = jnp.max(hit.reshape(ROWS, COLS, LANES), axis=1)
        rank = jnp.dot(need.astype(jnp.float32), before, preferred_element_type=jnp.float32)
        return need, rank.astype(jnp.int32)

    info_ref[...] = jnp.zeros((INFO, LANES), jnp.int32)
    for q in range(ROWS * KB // LANES):
        need, rank = needed(q * LANES)
        owner = (lane8 + q * LANES) // KB
        top = jnp.maximum(top, jnp.where(owner == sub8, 0, need + rank))
        mine = jnp.sum(jnp.where(sub8 == me_r, rank, 0), axis=0, keepdims=True)
        info_ref[RANK + q:RANK + q + 1, :] = mine
    largest = jnp.max(top)
    which_ref[0] = sum((largest > cap).astype(jnp.int32) for cap in CAPS)
    info_ref[MISC:MISC + 1, :] = jnp.where(
        lane8[0:1] == 0, largest, jnp.where(lane8[0:1] == 1, me_r, me_c))

    need, rank = needed(me_r * KB)
    need = jnp.where((lane8 < KB) & (sub8 != me_r), need, 0)
    counts = jnp.sum(need, axis=1, keepdims=True)

    def place(s, lists):
        here = jnp.sum(jnp.where((need == 1) & (rank == s), lane8, 0), axis=1, keepdims=True)
        return jnp.where(lane8 == s, here, lists)

    lists = lax.fori_loop(0, largest, place, jnp.zeros((ROWS, LANES), jnp.int32))
    info_ref[SEND:SEND + ROWS, :] = jnp.where(lane8 == LANES - 1, counts, lists)
    for src in range(ROWS):
        info_ref[META + src:META + src + 1, :] = meta_ref[pl.ds(src * COLS + me_c, 1), :]
    info_ref[KEYS:KEYS + SLOTS, :] = meta_ref[pl.ds(pl.multiple_of(me_r * COLS, COLS), COLS), :]


def make_lists(me, meta):
    return pl.pallas_call(
        list_kernel,
        out_shape=(
            jax.ShapeDtypeStruct((INFO, LANES), jnp.int32),
            jax.ShapeDtypeStruct((1,), jnp.int32),
        ),
        in_specs=[
            pl.BlockSpec(memory_space=pltpu.SMEM),
            pl.BlockSpec(memory_space=pltpu.VMEM),
        ],
        out_specs=(
            pl.BlockSpec(memory_space=pltpu.VMEM),
            pl.BlockSpec(memory_space=pltpu.SMEM),
        ),
        name="make_lists",
    )(me, meta)


def pack_kernel(cap, first, info_ref, b_ref, out_ref, sems):
    def each(dest, go):
        count = jnp.minimum(info_ref[SEND + dest, LANES - 1] - first, cap)

        @pl.loop(0, count)
        def _(s):
            block = info_ref[SEND + dest, first + s]
            go(pltpu.make_async_copy(b_ref.at[block], out_ref.at[dest, s], sems.at[dest, s]))

    @pl.loop(0, ROWS)
    def _(dest):
        each(dest, lambda copy: copy.start())

    @pl.loop(0, ROWS)
    def _(dest):
        each(dest, lambda copy: copy.wait())


def pack(cap, first, info, b):
    return pl.pallas_call(
        functools.partial(pack_kernel, cap, first),
        out_shape=jax.ShapeDtypeStruct((ROWS, cap, BS, BS), jnp.bfloat16),
        in_specs=[
            pl.BlockSpec(memory_space=pltpu.SMEM),
            pl.BlockSpec(memory_space=pltpu.VMEM),
        ],
        out_specs=pl.BlockSpec(memory_space=pl.ANY),
        scratch_shapes=[pltpu.SemaphoreType.DMA((ROWS, cap))],
        compiler_params=pltpu.CompilerParams(vmem_limit_bytes=8 << 20),
        name="pack_blocks",
    )(info, b)


def plan_kernel(info_ref, mask_ref, plan_ref, head_of):
    me_r, me_c = info_ref[MISC, 1], info_ref[MISC, 2]

    @pl.loop(0, RB)
    def _(i):
        @pl.loop(0, JB)
        def _(j):
            head_of[j] = -1

        plan_ref[i, COUNT] = 0

        @pl.loop(0, SLOTS)
        def _(a):
            key = info_ref[KEYS + a, i]

            @pl.when(key >= 0)
            def _():
                src, block = key // KB, lax.rem(key, KB)
                col = info_ref[META + src, RB + block]

                @pl.when(mask_ref[i, col] != 0)
                def _():
                    n = plan_ref[i, COUNT]
                    head = head_of[col]
                    rank = info_ref[RANK + key // LANES, lax.rem(key, LANES)]
                    part = (a ^ me_c) & 1
                    shift = ((me_c >> 1) - (a >> 1)) & 3
                    turn = ((a ^ me_c) >> 3) & 1
                    plan_ref[i, LEFT + n] = (part * 4 + shift) * 2 + turn
                    plan_ref[i, SOURCE + n] = jnp.where(src == me_r, -1, src)
                    plan_ref[i, PLACE + n] = jnp.where(src == me_r, block, rank)
                    plan_ref[i, COL + n] = col
                    plan_ref[i, HEAD + n] = jnp.where(head < 0, n, head)
                    plan_ref[i, COUNT] = n + 1

                    @pl.when(head < 0)
                    def _():
                        head_of[col] = n


def make_plan(info, mask):
    return pl.pallas_call(
        plan_kernel,
        out_shape=jax.ShapeDtypeStruct((RB, LANES), jnp.int32),
        in_specs=[
            pl.BlockSpec(memory_space=pltpu.SMEM),
            pl.BlockSpec(memory_space=pltpu.SMEM),
        ],
        out_specs=pl.BlockSpec(memory_space=pltpu.SMEM),
        scratch_shapes=[pltpu.SMEM((JB,), jnp.int32)],
        cost_estimate=pl.CostEstimate(flops=0, bytes_accessed=8 << 20, transcendentals=0),
        name="make_plan",
    )(info, mask)


def zero_kernel(info_ref, out_ref, zeros, sems):
    zeros[...] = jnp.zeros(zeros.shape, zeros.dtype)
    copies = [
        pltpu.make_async_copy(zeros, out_ref.at[i], sems.at[i]) for i in range(RB)
    ]
    for copy in copies:
        copy.start()
    for copy in copies:
        copy.wait()


def zero_blocks(info):
    return pl.pallas_call(
        zero_kernel,
        out_shape=jax.ShapeDtypeStruct((RB, JB, BS, BS), jnp.bfloat16),
        in_specs=[pl.BlockSpec(memory_space=pl.ANY)],
        out_specs=pl.BlockSpec(memory_space=pl.ANY),
        scratch_shapes=[
            pltpu.VMEM((JB, BS, BS), jnp.bfloat16),
            pltpu.SemaphoreType.DMA((RB,)),
        ],
        compiler_params=pltpu.CompilerParams(vmem_limit_bytes=8 << 20),
        cost_estimate=pl.CostEstimate(flops=0, bytes_accessed=16 << 20, transcendentals=0),
        name="zero_blocks",
    )(info)


def product_kernel(plan_ref, *refs):
    left_refs, (got_ref, b_ref, _, out_ref) = refs[:8], refs[8:12]
    a_buf, b_buf, res, acc, a_sems, b_sems, out_sems = refs[12:]

    for n, ref in enumerate(left_refs):
        pltpu.make_async_copy(ref, a_buf.at[pl.ds(2 * n, 2)], a_sems.at[n]).start()

    @pl.loop(0, RB)
    def _(i):
        @pl.loop(0, plan_ref[i, COUNT])
        def _(n):
            src, place = plan_ref[i, SOURCE + n], plan_ref[i, PLACE + n]

            @pl.when(src < 0)
            def _():
                pltpu.make_async_copy(b_ref.at[place], b_buf.at[i, n], b_sems.at[i, n]).start()

            @pl.when(src >= 0)
            def _():
                pltpu.make_async_copy(got_ref.at[src, place], b_buf.at[i, n], b_sems.at[i, n]).start()

    for n, ref in enumerate(left_refs):
        pltpu.make_async_copy(ref, a_buf.at[pl.ds(2 * n, 2)], a_sems.at[n]).wait()

    def write(i, n):
        return pltpu.make_async_copy(res.at[i, n], out_ref.at[i, plan_ref[i, COL + n]], out_sems.at[i, n])

    @pl.loop(0, RB)
    def _(i):
        count = plan_ref[i, COUNT]

        @pl.loop(0, (count + UNROLL - 1) // UNROLL)
        def _(step):
            sums = []
            for u in range(UNROLL):
                n = step * UNROLL + u
                within = n < count

                @pl.when(within)
                def _():
                    pltpu.make_async_copy(b_ref.at[0], b_buf.at[i, n], b_sems.at[i, n]).wait()

                left = jnp.where(within, plan_ref[i, LEFT + n], 0)
                head = jnp.where(within, plan_ref[i, HEAD + n], SLOTS)
                sums.append((n, head, jnp.dot(
                    a_buf[left, i], b_buf[i, n], preferred_element_type=jnp.float32)))
            for n, head, total in sums:
                total = total + jnp.where(head != n, acc[head], 0.0)
                acc[head] = total
                res[i, head] = total.astype(jnp.bfloat16)

        @pl.loop(0, count)
        def _(n):
            @pl.when(plan_ref[i, HEAD + n] == n)
            def _():
                write(i, n).start()

    @pl.loop(0, RB)
    def _(i):
        @pl.loop(0, plan_ref[i, COUNT])
        def _(n):
            @pl.when(plan_ref[i, HEAD + n] == n)
            def _():
                write(i, n).wait()


def products(plan, left, got, b, blank):
    return pl.pallas_call(
        product_kernel,
        out_shape=jax.ShapeDtypeStruct((RB, JB, BS, BS), jnp.bfloat16),
        in_specs=[pl.BlockSpec(memory_space=pltpu.SMEM)] + [pl.BlockSpec(memory_space=pl.ANY)] * 11,
        out_specs=pl.BlockSpec(memory_space=pl.ANY),
        input_output_aliases={11: 0},
        scratch_shapes=[
            pltpu.VMEM((SLOTS, RB, BS, BS), jnp.bfloat16),
            pltpu.VMEM((RB, SLOTS, BS, BS), jnp.bfloat16),
            pltpu.VMEM((RB, SLOTS + 1, BS, BS), jnp.bfloat16),
            pltpu.VMEM((SLOTS + 1, BS, BS), jnp.float32),
            pltpu.SemaphoreType.DMA((8,)),
            pltpu.SemaphoreType.DMA((RB, SLOTS)),
            pltpu.SemaphoreType.DMA((RB, SLOTS)),
        ],
        compiler_params=pltpu.CompilerParams(vmem_limit_bytes=24 << 20),
        name="block_products",
    )(plan, *left, got, b, blank)


def per_device(a_values, a_blocks, a_live, b_values, b_columns, filter_mask):
    me_r, me_c = lax.axis_index(R_AXES), lax.axis_index(C_AXES)
    keys = jnp.where(a_live != 0, a_blocks, -1)[:, 0]
    record = jnp.concatenate([keys, b_columns[:, 0] - me_c * JB])
    record = jnp.pad(record, (0, LANES - record.shape[0]))
    meta = lax.all_to_all(
        jnp.broadcast_to(record[None, :], (ROWS * COLS, LANES)), R_AXES + C_AXES, 0, 0, tiled=True)
    a = a_values.reshape(RB, BS, BS)
    b = b_values.reshape(KB, BS, BS)
    across = lax.ppermute(a, "zh", [(0, 1), (1, 0)])
    info, which = make_lists(jnp.stack([me_r, me_c]).astype(jnp.int32), meta)

    def exchange(cap, first, info, b):
        return lax.all_to_all(pack(cap, first, info, b), R_AXES, 0, 0)

    def finish(info, mask, a, across, b, got):
        pair = jnp.stack([a, across])
        along = [pair] + [
            lax.ppermute(pair, "x", [(i, (i + s) % 4) for i in range(4)]) for s in range(1, 4)]
        left = along + [lax.ppermute(part, "core", [(0, 1), (1, 0)]) for part in along]
        return products(make_plan(info, mask), left, got, b, zero_blocks(info))

    def one_round(cap, info, mask, a, across, b):
        packed = pack(cap, 0, info, b)
        packed, a, across, info = lax.optimization_barrier((packed, a, across, info))
        got = lax.all_to_all(packed, R_AXES, 0, 0)
        return finish(info, mask, a, across, b, got)

    def rounds(info, mask, a, across, b):
        cap = CAPS[-1]
        got = [exchange(cap, first, info, b) for first in range(0, KB, cap)]
        return finish(info, mask, a, across, b, jnp.concatenate(got, axis=1))

    branches = [functools.partial(one_round, cap) for cap in CAPS] + [rounds]
    return lax.switch(which[0], branches, info, filter_mask, a, across, b)


def solution(mesh):
    fine = Mesh(mesh.devices.reshape(4, 2, 2, 4, 2), R_AXES + C_AXES)
    pair = P(R_AXES, C_AXES)
    blocks = P(R_AXES, C_AXES, None, None)
    return jax.shard_map(
        per_device, mesh=fine, in_specs=(blocks, pair, pair, blocks, pair, pair),
        out_specs=blocks, check_vma=False
    )
```

time: 558 us -> 105 us (0.19)
  waiting for transfers between devices: 330 us -> 35 us
  local copies, waits for them, and re-layouts: 97.1 us -> 3.88 us
  blocking collectives: 55.5 us -> 0 us
  matrix products: 40.7 us -> 0 us
  Pallas kernels: 0 us -> 36.7 us
  starting transfers between devices: 0.04 us -> 25.7 us
  other arithmetic: 19.8 us -> 2.11 us
  between operations: 14.1 us -> 0.91 us
    all_gather x2 -> x0, waiting for transfers between devices: 328 us -> none  [the longest x1 326 us: per_device(): lax.all_gather(b_values, 'row', axis=0, tiled=True)]
    gather x16 -> x0, local copies, waits for them, and re-layouts: 55.8 us -> none  [the longest x8 51.3 us: one_row(): chosen = b_all[blocks_row]]
    all_gather x2 -> x0, blocking collectives: 45.6 us -> none  [the longest x1 26.4 us: per_device(): lax.all_gather(a_blocks, 'col', axis=1, tiled=True)]
    dot_general x16 -> x0, matrix products: 40.7 us -> none  [the longest x8 28.2 us: one_row(): jnp.einsum('abj,abmp->jmp', weights, products, precision=lax.Precision.HI...]
    pallas_call x0 -> x5, Pallas kernels: none -> 36.7 us  [the longest x1 10.8 us: make_plan(): pl.pallas_call(plan_kernel, out_shape=jax.ShapeDtypeStruct((RB, LANES), j...]
    dynamic_update_slice x8 -> x0, local copies, waits for them, and re-layouts: 35 us -> none  [per_device(): summed = lax.map(one_row, (all_values, all_blocks, all_alive))]
    ppermute x0 -> x8, waiting for transfers between devices: none -> 19 us  [the longest x3 19 us: finish(): lax.ppermute(pair, 'x', [(i, (i + s) % 4) for i in range(4)])]
    convert_element_type x10 -> x0, other arithmetic: 18.6 us -> none  [the longest x1 17.8 us: per_device(): (summed * filter_mask.astype(jnp.float32)[:, :, None, None]).astype(jnp.b...]
  transfers between devices with their start and end apart: 2 -> 10, of which waited for: 2 -> 4; matrix products, arithmetic and copies ran while one was open for 1% -> 3% of each run, Pallas kernels for 0% -> 19%
where the time goes in v1:
time: 105 us
  Pallas kernels  36.7 us (35%)
  waiting for transfers between devices  35 us (33%)
  starting transfers between devices  25.7 us (24%)
  local copies, waits for them, and re-layouts  3.88 us (4%)
  other arithmetic  2.11 us (2%)
    ppermute x3, waiting for transfers between devices, finish(): lax.ppermute(pair, 'x', [(i, (i + s) % 4) for i in range(4)])  19 us
    pallas_call x1, Pallas kernels, make_plan(): pl.pallas_call(plan_kernel, out_shape=jax.ShapeDtypeStruct((RB, LANES), j...  10.8 us
    pallas_call x1, Pallas kernels, products(): pl.pallas_call(product_kernel, out_shape=jax.ShapeDtypeStruct((RB, JB, BS...  10.2 us
    all_to_all x1, waiting for transfers between devices, per_device(): lax.all_to_all(jnp.broadcast_to(record[None, :], (ROWS * COLS, LANES)), R...  9.05 us
    all_to_all x1, starting transfers between devices, per_device(): lax.all_to_all(jnp.broadcast_to(record[None, :], (ROWS * COLS, LANES)), R...  7.93 us
    all_to_all x1, waiting for transfers between devices, one_round(): got = lax.all_to_all(packed, R_AXES, 0, 0)  6.95 us
    ppermute x4, starting transfers between devices, finish(): lax.ppermute(part, 'core', [(0, 1), (1, 0)])  6.74 us
    pallas_call x1, Pallas kernels, zero_blocks(): pl.pallas_call(zero_kernel, out_shape=jax.ShapeDtypeStruct((RB, JB, BS, B...  6.19 us
  transfers between devices with their start and end apart: 10, of which 4 were waited for; matrix products, arithmetic and copies ran while one was open for 3% of the time, Pallas kernels for 19%

profile of v1, /device:TPU:1, one launch (start us, length us, event | category | flops | bytes accessed | tf_op | source)
XLA Modules:
  0.0 104.9 jit_solution(14836160420003229378)
XLA Ops:
  0.0 4.4 %collective-permute-start.42 = (bf16[8,128,128]{2,1,0:T(8,128)(2,1)}, bf16[8,128,128]{2,1,0:T(8,128)(2,1)}, u32[]{:S(2)}, u32[]{:S(2)}) collective-permute-start(bf16[8,128,128]{2,1,0:T(8,128)(2,1)} %bitcast.29), channel_id=1, source_target_pairs={{0,8},{8,0},{1,9},{9,1},{2,10},{10,2},{3,11},{11,3},{4,12},{12,4},... | collective-permute-start | bytes 786440 | tf_op jit(solution)/shard_map/ppermute | solution.py:308
  4.4 0.7 fusion
  5.1 0.7 subtract_bitcast_fusion
  5.8 0.1 pad_add_fusion.1
  5.8 0.7 broadcast_in_dim.11
  6.5 7.9 %all-to-all-start.9 = ((s32[128,1,128]{2,1,0:T(1,128)}), s32[128,1,128]{2,1,0:T(1,128)S(1)}, u32[]{:S(2)}, u32[]{:S(2)}) async-start(s32[128,1,128]{2,1,0:T(1,128)} %broadcast_in_dim.11), calls=%async_computation.9 | async-start | bytes 131072 | tf_op jit(solution)/shard_map/all_to_all | solution.py:304
  14.5 0.7 pad_add_fusion.me_ref
  15.1 9.0 %all-to-all-done.9 = s32[128,1,128]{2,1,0:T(1,128)S(1)} async-done(((s32[128,1,128]{2,1,0:T(1,128)}), s32[128,1,128]{2,1,0:T(1,128)S(1)}, u32[]{:S(2)}, u32[]{:S(2)}) %all-to-all-start.9) | async-done | bytes 65568 | tf_op jit(solution)/shard_map/all_to_all | solution.py:304
  24.2 0.6 copy-done.28
  24.8 3.3 %make_lists.1 = (s32[40,128]{1,0:T(8,128)S(1)}, s32[1]{0:T(128)}) custom-call(s32[2]{0:T(128)} %pad_add_fusion.me_ref, s32[128,128]{1,0:T(8,128)} %bitcast.47), custom_call_target="tpu_custom_call" | custom-call | tf_op jit(solution)/shard_map/make_lists/pallas_call | solution.py:79
  28.8 76.0 %conditional.1 = (bf16[8,64,128,128]{3,2,1,0:T(8,128)(2,1)}) conditional(s32[]{:T(128)} %bitcast.18, (s32[40,128]{1,0:T(8,128)S(1)}, bf16[64,128,128]{2,1,0:T(8,128)(2,1)}, bf16[8,128,128]{2,1,0:T(8,128)(2,1)}, bf16[8,128,128]{2,1,0:T(8,128)(2,1)}, s32[8,64]{1,0:T(8,128)}) %tuple.50, (s32[40,128]{1,0:T(8,128)S(1)}, ...), branch_computations={%region_0.1_spmd, %region_1.2_spmd, %region_2.3_spmd, %region_3.4_... | conditional | flops 31719424 | bytes 332423904 | solution.py:333
  28.8 0.0 copy-start.18
  28.8 6.1 %pack_blocks.10 = bf16[8,14,128,128]{3,2,1,0:T(8,128)(2,1)S(1)} custom-call(s32[40,128]{1,0:T(8,128)S(1)} %get-tuple-element.85.info_ref, bf16[64,128,128]{2,1,0:T(8,128)(2,1)} %get-tuple-element.82.b_ref.refs_9_), custom_call_target="tpu_custom_call" | custom-call | tf_op jit(solution)/shard_map/cond/branch_1_fun/pack_blocks/pallas_call | solution.py:116
  35.0 1.9 %copy-done.8 = bf16[8,14,128,128]{3,2,1,0:T(8,128)(2,1)} copy-done((bf16[8,14,128,128]{3,2,1,0:T(8,128)(2,1)}, bf16[8,14,128,128]{3,2,1,0:T(8,128)(2,1)S(1)}, u32[]{:S(2)}) %copy-start.8) | copy-done | bytes 3670040 | tf_op jit(solution)/shard_map/cond
  36.8 4.5 %all-to-all-start.1 = ((bf16[8,14,128,128]{3,2,1,0:T(8,128)(2,1)}), bf16[8,14,128,128]{3,2,1,0:T(8,128)(2,1)}, u32[]{:S(2)}, u32[]{:S(2)}) async-start(bf16[8,14,128,128]{3,2,1,0:T(8,128)(2,1)} %copy-done.8), calls=%async_computation.1 | async-start | bytes 7340032 | tf_op jit(solution)/shard_map/cond/branch_1_fun/all_to_all | solution.py:324
  41.4 0.1 pad_maximum_fusion.1.refs_0_
  41.4 0.0 copy-start.30
  41.4 0.8 collective-permute-start.9
  42.3 1.3 %collective-permute-start.8 = (bf16[2,8,128,128]{3,2,1,0:T(8,128)(2,1)S(1)}, bf16[2,8,128,128]{3,2,1,0:T(8,128)(2,1)S(1)}, u32[]{:S(2)}, u32[]{:S(2)}) collective-permute-start(bf16[2,8,128,128]{3,2,1,0:T(8,128)(2,1)S(1)} %pad_maximum_fusion.1.refs_0_), channel_id=1, source_target_pairs={{0,4},{2,6},{4,0},{6,2},{1,5},{3,7},{5,1},{7,3},{8,12},{10,14},{12... | collective-permute-start | bytes 1572872 | tf_op jit(solution)/shard_map/cond/branch_1_fun/ppermute | solution.py:317
  43.6 0.0 collective-permute-start.7
  43.6 1.3 %collective-permute-start.10 = (bf16[2,8,128,128]{3,2,1,0:T(8,128)(2,1)S(1)}, bf16[2,8,128,128]{3,2,1,0:T(8,128)(2,1)S(1)}, u32[]{:S(2)}, u32[]{:S(2)}) collective-permute-start(bf16[2,8,128,128]{3,2,1,0:T(8,128)(2,1)S(1)} %pad_maximum_fusion.1.refs_0_), channel_id=1, source_target_pairs={{0,1},{1,0},{2,3},{3,2},{4,5},{5,4},{6,7},{7,6},{8,9},{9,8},{10,11... | collective-permute-start | bytes 1572872 | tf_op jit(solution)/shard_map/cond/branch_1_fun/ppermute | solution.py:318
  44.9 9.6 %collective-permute-done.9.refs_3_ = bf16[2,8,128,128]{3,2,1,0:T(8,128)(2,1)S(1)} collective-permute-done((bf16[2,8,128,128]{3,2,1,0:T(8,128)(2,1)S(1)}, bf16[2,8,128,128]{3,2,1,0:T(8,128)(2,1)S(1)}, u32[]{:S(2)}, u32[]{:S(2)}) %collective-permute-start.9) | collective-permute-done | bytes 524320 | tf_op jit(solution)/shard_map/cond/branch_1_fun/ppermute | solution.py:317
  54.5 2.4 %collective-permute-start.13 = (bf16[2,8,128,128]{3,2,1,0:T(8,128)(2,1)S(1)}, bf16[2,8,128,128]{3,2,1,0:T(8,128)(2,1)S(1)}, u32[]{:S(2)}, u32[]{:S(2)}) collective-permute-start(bf16[2,8,128,128]{3,2,1,0:T(8,128)(2,1)S(1)} %collective-permute-done.9.refs_3_), channel_id=1, source_target_pairs={{0,1},{1,0},{2,3},{3,2},{4,5},{5,4},{6,7},{7,6},{8,9},{9,8},{10,11... | collective-permute-start | bytes 1572872 | tf_op jit(solution)/shard_map/cond/branch_1_fun/ppermute | solution.py:318
  56.9 0.0 collective-permute-done.8.refs_2_
  56.9 2.6 %collective-permute-start.12 = (bf16[2,8,128,128]{3,2,1,0:T(8,128)(2,1)S(1)}, bf16[2,8,128,128]{3,2,1,0:T(8,128)(2,1)}, u32[]{:S(2)}, u32[]{:S(2)}) collective-permute-start(bf16[2,8,128,128]{3,2,1,0:T(8,128)(2,1)S(1)} %collective-permute-done.8.refs_2_), channel_id=1, source_target_pairs={{0,1},{1,0},{2,3},{3,2},{4,5},{5,4},{6,7},{7,6},{8,9},{9,8},{10,11... | collective-permute-start | bytes 1572872 | tf_op jit(solution)/shard_map/cond/branch_1_fun/ppermute | solution.py:318
  59.5 9.4 %collective-permute-done.7.refs_1_ = bf16[2,8,128,128]{3,2,1,0:T(8,128)(2,1)S(1)} collective-permute-done((bf16[2,8,128,128]{3,2,1,0:T(8,128)(2,1)S(1)}, bf16[2,8,128,128]{3,2,1,0:T(8,128)(2,1)S(1)}, u32[]{:S(2)}, u32[]{:S(2)}) %collective-permute-start.7) | collective-permute-done | bytes 524320 | tf_op jit(solution)/shard_map/cond/branch_1_fun/ppermute | solution.py:317
  68.9 0.4 collective-permute-start.11
  69.3 6.2 %zero_blocks.7.refs_10_ = bf16[8,64,128,128]{3,2,1,0:T(8,128)(2,1)} custom-call(s32[40,128]{1,0:T(8,128)S(1)} %get-tuple-element.85.info_ref), custom_call_target="tpu_custom_call" | custom-call | bytes 16777216 | tf_op jit(solution)/shard_map/cond/branch_1_fun/zero_blocks/pallas_call | solution.py:197
  75.5 10.8 %make_plan.7.plan_ref = s32[8,128]{1,0:T(8,128)} custom-call(s32[40,128]{1,0:T(8,128)S(1)} %get-tuple-element.85.info_ref, s32[8,64]{1,0:T(8,128)S(1)} %copy-done.30), custom_call_target="tpu_custom_call" | custom-call | bytes 8388608 | tf_op jit(solution)/shard_map/cond/branch_1_fun/make_plan/pallas_call | solution.py:171
  86.4 6.9 %all-to-all-done.1.refs_8_ = bf16[8,14,128,128]{3,2,1,0:T(8,128)(2,1)} async-done(((bf16[8,14,128,128]{3,2,1,0:T(8,128)(2,1)}), bf16[8,14,128,128]{3,2,1,0:T(8,128)(2,1)}, u32[]{:S(2)}, u32[]{:S(2)}) %all-to-all-start.1) | async-done | bytes 3670048 | tf_op jit(solution)/shard_map/cond/branch_1_fun/all_to_all | solution.py:324
  93.4 0.7 copy-done.11
  94.1 10.2 %block_products.7 = bf16[8,64,128,128]{3,2,1,0:T(8,128)(2,1)} custom-call(s32[8,128]{1,0:T(8,128)S(1)} %copy-done.11, bf16[2,8,128,128]{3,2,1,0:T(8,128)(2,1)S(1)} %pad_maximum_fusion.1.refs_0_, bf16[2,8,128,128]{3,2,1,0:T(8,128)(2,1)S(1)} %collective-permute-done.7.refs_1_, ...), custom_call_target="tpu_custom_call", output_to_operand_aliasing={{}: (11, {})} | custom-call | tf_op jit(solution)/shard_map/cond/branch_1_fun/block_products/pallas_call | solution.py:279
  (13 shorter events, 0.0 us)
Async XLA Ops:
  0.0 28.8 %collective-permute-start.42 = (bf16[8,128,128]{2,1,0:T(8,128)(2,1)}, bf16[8,128,128]{2,1,0:T(8,128)(2,1)}, u32[]{:S(2)}, u32[]{:S(2)}) collective-permute-start(bf16[8,128,128]{2,1,0:T(8,128)(2,1)} %bitcast.29), channel_id=1, source_target_pairs={{0,8},{8,0},{1,9},{9,1},{2,10},{10,2},{3,11},{11,3},{4,12},{12,4},... | collective-permute-start | bytes 786440 | tf_op jit(solution)/shard_map/ppermute | solution.py:308
  6.5 17.6 %all-to-all-start.9 = ((s32[128,1,128]{2,1,0:T(1,128)}), s32[128,1,128]{2,1,0:T(1,128)S(1)}, u32[]{:S(2)}, u32[]{:S(2)}) async-start(s32[128,1,128]{2,1,0:T(1,128)} %broadcast_in_dim.11), calls=%async_computation.9 | async-start | bytes 131072 | tf_op jit(solution)/shard_map/all_to_all | solution.py:304
  24.2 0.6 copy-start.28
  28.8 12.5 %copy-start.18 = (bf16[8,128,128]{2,1,0:T(8,128)(2,1)S(1)}, bf16[8,128,128]{2,1,0:T(8,128)(2,1)}, u32[]{:S(2)}) copy-start(bf16[8,128,128]{2,1,0:T(8,128)(2,1)} %get-tuple-element.87) | copy-start | bytes 786436 | tf_op jit(solution)/shard_map/cond
  28.8 12.5 %copy-start.23 = (bf16[8,128,128]{2,1,0:T(8,128)(2,1)S(1)}, bf16[8,128,128]{2,1,0:T(8,128)(2,1)}, u32[]{:S(2)}) copy-start(bf16[8,128,128]{2,1,0:T(8,128)(2,1)} %get-tuple-element.88) | copy-start | bytes 786436 | tf_op jit(solution)/shard_map/cond
  35.0 1.9 %copy-start.8 = (bf16[8,14,128,128]{3,2,1,0:T(8,128)(2,1)}, bf16[8,14,128,128]{3,2,1,0:T(8,128)(2,1)S(1)}, u32[]{:S(2)}) copy-start(bf16[8,14,128,128]{3,2,1,0:T(8,128)(2,1)S(1)} %pack_blocks.10) | copy-start | bytes 11010052 | tf_op jit(solution)/shard_map/cond
  36.8 56.5 %all-to-all-start.1 = ((bf16[8,14,128,128]{3,2,1,0:T(8,128)(2,1)}), bf16[8,14,128,128]{3,2,1,0:T(8,128)(2,1)}, u32[]{:S(2)}, u32[]{:S(2)}) async-start(bf16[8,14,128,128]{3,2,1,0:T(8,128)(2,1)} %copy-done.8), calls=%async_computation.1 | async-start | bytes 7340032 | tf_op jit(solution)/shard_map/cond/branch_1_fun/all_to_all | solution.py:324
  41.4 34.1 %copy-start.30 = (s32[8,64]{1,0:T(8,128)S(1)}, s32[8,64]{1,0:T(8,128)}, u32[]{:S(2)}) copy-start(s32[8,64]{1,0:T(8,128)} %get-tuple-element.86.mask_ref) | copy-start | bytes 6148 | tf_op jit(solution)/shard_map/cond
  41.4 13.0 %collective-permute-start.9 = (bf16[2,8,128,128]{3,2,1,0:T(8,128)(2,1)S(1)}, bf16[2,8,128,128]{3,2,1,0:T(8,128)(2,1)S(1)}, u32[]{:S(2)}, u32[]{:S(2)}) collective-permute-start(bf16[2,8,128,128]{3,2,1,0:T(8,128)(2,1)S(1)} %pad_maximum_fusion.1.refs_0_), channel_id=1, source_target_pairs={{0,6},{2,0},{4,2},{6,4},{1,7},{3,1},{5,3},{7,5},{8,14},{10,8},{12,... | collective-permute-start | bytes 1572872 | tf_op jit(solution)/shard_map/cond/branch_1_fun/ppermute | solution.py:317
  42.3 14.7 %collective-permute-start.8 = (bf16[2,8,128,128]{3,2,1,0:T(8,128)(2,1)S(1)}, bf16[2,8,128,128]{3,2,1,0:T(8,128)(2,1)S(1)}, u32[]{:S(2)}, u32[]{:S(2)}) collective-permute-start(bf16[2,8,128,128]{3,2,1,0:T(8,128)(2,1)S(1)} %pad_maximum_fusion.1.refs_0_), channel_id=1, source_target_pairs={{0,4},{2,6},{4,0},{6,2},{1,5},{3,7},{5,1},{7,3},{8,12},{10,14},{12... | collective-permute-start | bytes 1572872 | tf_op jit(solution)/shard_map/cond/branch_1_fun/ppermute | solution.py:317
  43.6 25.4 %collective-permute-start.7 = (bf16[2,8,128,128]{3,2,1,0:T(8,128)(2,1)S(1)}, bf16[2,8,128,128]{3,2,1,0:T(8,128)(2,1)S(1)}, u32[]{:S(2)}, u32[]{:S(2)}) collective-permute-start(bf16[2,8,128,128]{3,2,1,0:T(8,128)(2,1)S(1)} %pad_maximum_fusion.1.refs_0_), channel_id=1, source_target_pairs={{0,2},{2,4},{4,6},{6,0},{1,3},{3,5},{5,7},{7,1},{8,10},{10,12},{12... | collective-permute-start | bytes 1572872 | tf_op jit(solution)/shard_map/cond/branch_1_fun/ppermute | solution.py:317
  43.6 42.8 %collective-permute-start.10 = (bf16[2,8,128,128]{3,2,1,0:T(8,128)(2,1)S(1)}, bf16[2,8,128,128]{3,2,1,0:T(8,128)(2,1)S(1)}, u32[]{:S(2)}, u32[]{:S(2)}) collective-permute-start(bf16[2,8,128,128]{3,2,1,0:T(8,128)(2,1)S(1)} %pad_maximum_fusion.1.refs_0_), channel_id=1, source_target_pairs={{0,1},{1,0},{2,3},{3,2},{4,5},{5,4},{6,7},{7,6},{8,9},{9,8},{10,11... | collective-permute-start | bytes 1572872 | tf_op jit(solution)/shard_map/cond/branch_1_fun/ppermute | solution.py:318
  54.5 31.9 %collective-permute-start.13 = (bf16[2,8,128,128]{3,2,1,0:T(8,128)(2,1)S(1)}, bf16[2,8,128,128]{3,2,1,0:T(8,128)(2,1)S(1)}, u32[]{:S(2)}, u32[]{:S(2)}) collective-permute-start(bf16[2,8,128,128]{3,2,1,0:T(8,128)(2,1)S(1)} %collective-permute-done.9.refs_3_), channel_id=1, source_target_pairs={{0,1},{1,0},{2,3},{3,2},{4,5},{5,4},{6,7},{7,6},{8,9},{9,8},{10,11... | collective-permute-start | bytes 1572872 | tf_op jit(solution)/shard_map/cond/branch_1_fun/ppermute | solution.py:318
  56.9 29.5 %collective-permute-start.12 = (bf16[2,8,128,128]{3,2,1,0:T(8,128)(2,1)S(1)}, bf16[2,8,128,128]{3,2,1,0:T(8,128)(2,1)}, u32[]{:S(2)}, u32[]{:S(2)}) collective-permute-start(bf16[2,8,128,128]{3,2,1,0:T(8,128)(2,1)S(1)} %collective-permute-done.8.refs_2_), channel_id=1, source_target_pairs={{0,1},{1,0},{2,3},{3,2},{4,5},{5,4},{6,7},{7,6},{8,9},{9,8},{10,11... | collective-permute-start | bytes 1572872 | tf_op jit(solution)/shard_map/cond/branch_1_fun/ppermute | solution.py:318
  68.9 17.5 %collective-permute-start.11 = (bf16[2,8,128,128]{3,2,1,0:T(8,128)(2,1)S(1)}, bf16[2,8,128,128]{3,2,1,0:T(8,128)(2,1)}, u32[]{:S(2)}, u32[]{:S(2)}) collective-permute-start(bf16[2,8,128,128]{3,2,1,0:T(8,128)(2,1)S(1)} %collective-permute-done.7.refs_1_), channel_id=1, source_target_pairs={{0,1},{1,0},{2,3},{3,2},{4,5},{5,4},{6,7},{7,6},{8,9},{9,8},{10,11... | collective-permute-start | bytes 1572872 | tf_op jit(solution)/shard_map/cond/branch_1_fun/ppermute | solution.py:318
  93.4 0.7 copy-start.11
